TPU v7x, 256 devices: a whole 4x4x8 slice. The times are simulated.
256 devices in a mesh: ctx: 32 (over z, x), head: 8 (over y, core).
Axes of the slice: x: 4, y: 4, z: 8, core: 2. Of those that a mesh axis runs over, the one named last changes fastest.
Arguments:
- hidden_rows: bfloat16 [8192, 8192], P('ctx', 'head'), may hold values from -6 to 6
- kv_weight: bfloat16 [8192, 2048], P(None, 'head'), may hold values from -0.0625 to 0.0625
- queries: bfloat16 [8192, 8192], P('ctx', 'head')
- kv_pool: bfloat16 [16384, 2048], P('ctx', 'head'), may hold values from -6 to 6
- slot_span: int32 [32], replicated, may hold values from 0 to 31, each once
- span_place: int32 [32], replicated, may hold values from 0 to 15, as said below
- row_index: int32 [32, 256], replicated, may hold values from 0 to 511, as said below
- block_count: int32 [32], replicated, may hold values from 1 to 2, as said below
Outputs:
- fresh_kv: bfloat16 [8192, 2048], P('ctx', 'head')
- attended: bfloat16 [8192, 8192], P('ctx', 'head')
Inputs may be any that keep to these rules, and one draw needn't show every extreme that they name: Owner o holds span slot_span[o]; each span is held by exactly one owner. `span_place`: within each request every position 0 to 15 is taken by exactly one span. Spans 0, 1 and 16 stand at positions 0, 1 and 2 of request 0. `row_index`: within each span the entries are distinct and increasing. `block_count`: some span has 2 blocks and some has 1.
All inputs are finite; a program needn't handle non-finite values.
Results may differ from a plain program's by a relative error of at most 0.01.
The roundings to bfloat16 on the way count: a program that leaves them out, or rounds other values in their place, can miss the bound.
Values may be sent and summed in bfloat16 or wider, within the bound.
No kernel may reach another device: no remote copies, remote signals or barrier semaphores. Data moves between devices by JAX's collectives and lax.ppermute only.
A program may use at most 64 MiB of HBM per device.

v0:
```python
import math

import jax
import jax.numpy as jnp
from jax import lax
from jax.sharding import PartitionSpec as P

BLK = 128


def rope_freqs(size):
    half = size // 2
    base = 500000.0 ** (-2.0 * jnp.arange(half, dtype=jnp.float32) / size)
    wavelen = 2.0 * math.pi / base
    smooth = (8192.0 / wavelen - 1.0) / 3.0
    blended = (1.0 - smooth) * base / 8.0 + smooth * base
    return jnp.where(wavelen < 2048.0, base, jnp.where(wavelen > 8192.0, base / 8.0, blended))


def rotate_keys(keys, positions):
    half = keys.shape[-1] // 2
    freqs = rope_freqs(keys.shape[-1])
    angles = positions.astype(jnp.float32)[:, None] * freqs[None, :]
    cosine = jnp.cos(angles)
    sine = jnp.sin(angles)
    first = keys[..., :half]
    second = keys[..., half:]
    return jnp.concatenate(
        [first * cosine - second * sine, second * cosine + first * sine], axis=-1
    )


def attend(state, query_blocks, query_pos, query_live, keys, vals, key_pos, key_usable):
    largest, total, accum = state
    scale = keys.shape[-1] ** (-0.5)
    scores = (
        jnp.einsum("rqd,nd->rqn", query_blocks, keys, preferred_element_type=jnp.float32) * scale
    )
    allowed = key_usable[None, :] & (key_pos[None, :] <= query_pos[:, None]) & query_live[:, None]
    masked = jnp.where(allowed[:, None, :], scores, -1e30)
    newest = jnp.maximum(largest, jnp.max(masked, axis=-1))
    factor = jnp.exp(largest - newest)
    weights = jnp.where(allowed[:, None, :], jnp.exp(scores - newest[..., None]), 0.0)
    total = total * factor + jnp.sum(weights, axis=-1)
    mixed = jnp.einsum(
        "rqn,nd->rqd", weights.astype(jnp.bfloat16), vals, preferred_element_type=jnp.float32
    )
    accum = accum * factor[..., None] + mixed
    return (newest, total, accum)


def keep_state(inner):
    return inner


def shards(hidden_rows, kv_weight, queries, kv_pool, slot_span, span_place, row_index, block_count):
    rows = hidden_rows.shape[0]
    width = kv_weight.shape[1] // 2
    heads = queries.shape[1] // width
    position = lax.axis_index("ctx")
    span_len = kv_pool.shape[0]
    projected = jnp.dot(
        lax.all_gather(hidden_rows, "head", axis=1, tiled=True),
        kv_weight,
        preferred_element_type=jnp.float32,
    )
    my_place = span_place[position]
    my_rows = lax.dynamic_index_in_dim(row_index, position, 0, keepdims=False)
    query_pos = my_place * span_len + my_rows
    query_live = jnp.arange(rows, dtype=jnp.int32) < block_count[position] * BLK
    fresh = jnp.concatenate(
        [rotate_keys(projected[:, :width], query_pos), projected[:, width:]], axis=1
    ).astype(jnp.bfloat16)
    query_blocks = queries.reshape(rows, heads, width)
    my_request = position // 2 % 2
    state = (
        jnp.full((rows, heads), -1e30, jnp.float32),
        jnp.zeros((rows, heads), jnp.float32),
        jnp.zeros((rows, heads, width), jnp.float32),
    )
    span_rows = jnp.arange(span_len, dtype=jnp.int32)
    live_table = jnp.arange(rows, dtype=jnp.int32)[None, :] < (block_count * BLK)[:, None]
    replaced = jnp.any(
        (row_index[:, :, None] == span_rows[None, None, :]) & live_table[:, :, None], axis=1
    )
    piece = lax.all_gather(fresh, "ctx", axis=0, tiled=True)
    count = piece.shape[0]
    block = math.gcd(count, rows)

    def step(index, inner):
        first = index * block
        span = first // rows
        within = first % rows
        place = span_place[span]
        visible = (span // 2 % 2 == my_request) & (place <= my_place)

        def attend_block(inner):
            rows_kv = lax.dynamic_slice_in_dim(piece, index * block, block, 0)
            span_rows_used = lax.dynamic_index_in_dim(row_index, span, 0, keepdims=False)
            key_pos = place * span_len + span_rows_used
            usable = within + jnp.arange(block, dtype=jnp.int32) < block_count[span] * BLK
            return attend(
                inner,
                query_blocks,
                query_pos,
                query_live,
                rows_kv[:, :width],
                rows_kv[:, width:],
                key_pos,
                usable,
            )

        return lax.cond(visible, attend_block, keep_state, inner)

    state = lax.fori_loop(0, count // block, step, state)
    over_piece = lax.all_gather(kv_pool, "ctx", axis=0, tiled=True)
    count = over_piece.shape[0]
    over_block = math.gcd(count, span_len)

    def step(index, inner):
        first = index * over_block
        owner = first // span_len
        within = first % span_len
        span = slot_span[owner]
        place = span_place[span]
        visible = (span // 2 % 2 == my_request) & (place <= my_place)

        def attend_block(inner):
            rows_kv = lax.dynamic_slice_in_dim(over_piece, index * over_block, over_block, 0)
            offsets = jnp.full((over_block,), place * span_len, jnp.int32)
            keys = rotate_keys(rows_kv[:, :width].astype(jnp.float32), offsets).astype(jnp.bfloat16)
            key_pos = place * span_len + within + jnp.arange(over_block, dtype=jnp.int32)
            span_replaced = lax.dynamic_index_in_dim(replaced, span, 0, keepdims=False)
            usable = jnp.logical_not(span_replaced)
            return attend(
                inner,
                query_blocks,
                query_pos,
                query_live,
                keys,
                rows_kv[:, width:],
                key_pos,
                usable,
            )

        return lax.cond(visible, attend_block, keep_state, inner)

    state = lax.fori_loop(0, count // over_block, step, state)
    largest, total, accum = state
    safe_total = jnp.where(query_live[:, None], total, 1.0)
    result = jnp.where(query_live[:, None, None], accum / safe_total[..., None], 0.0)
    return (fresh, result.reshape(rows, heads * width).astype(jnp.bfloat16))


def solution(mesh):
    in_specs = (
        P("ctx", "head"),
        P(None, "head"),
        P("ctx", "head"),
        P("ctx", "head"),
        P(),
        P(),
        P(),
        P(),
    )
    out_specs = (P("ctx", "head"), P("ctx", "head"))
    return jax.shard_map(shards, mesh=mesh, in_specs=in_specs, out_specs=out_specs, check_vma=False)
```

profile of v0, /device:TPU:70, one launch (start us, length us, event | category | flops | bytes accessed | tf_op | source)
XLA Modules:
  0.0 720.9 jit_solution(17852290639488574075)
XLA Ops:
  10.6 36.1 %all-gather.4.cloned.1.call-done = bf16[256,8192]{1,0:T(8,128)(2,1)} async-done(((bf16[256,1024]{1,0:T(8,128)(2,1)}), bf16[256,8192]{1,0:T(8,128)(2,1)}) %all-gather.4.cloned.1.call-update) | async-done | bytes 4194320 | tf_op jit(solution)/shard_map/all_gather | solution.py:63
  46.7 5.2 fusion.49
  60.3 75.5 %all-gather.6.cloned.1.call-done = bf16[8192,256]{0,1:T(8,128)(2,1)} async-done(((bf16[256,256]{0,1:T(8,128)(2,1)}), bf16[8192,256]{0,1:T(8,128)(2,1)}) %all-gather.6.cloned.1.call-update) | async-done | bytes 4194320 | tf_op jit(solution)/shard_map/all_gather | solution.py:86
  135.8 6.4 copy.26
  143.4 177.4 %while.42 = (s32[]{:T(128)}, f32[256,8]{0,1:T(8,128)S(1)}, f32[256,8]{0,1:T(8,128)S(1)}, f32[256,8,128]{2,0,1:T(8,128)}, s32[]{:T(128)}, /*index=5*/s32[32]{0:T(...) while((s32[]{:T(128)}, f32[256,8]{0,1:T(8,128)S(1)}, ...), condition=%wide.region_5.6_spmd.clone, body=%wide.region_0.5_spmd.clone.sunk | while | flops 274928704 | bytes 9445462 | solution.py:115
  149.6 7.0 conditional.6
  153.5 3.1 convolution_add_fusion
  158.6 7.0 conditional.6
  171.8 7.0 conditional.6
  180.8 7.0 conditional.6
  193.9 7.0 conditional.6
  197.8 3.2 convolution_add_fusion
  202.9 7.0 conditional.6
  206.8 3.1 convolution_add_fusion
  216.1 6.9 conditional.6
  225.1 7.0 conditional.6
  238.3 7.0 conditional.6
  242.1 3.1 convolution_add_fusion
  247.3 7.0 conditional.6
  251.1 3.1 convolution_add_fusion
  260.4 7.0 conditional.6
  264.3 3.1 convolution_add_fusion
  269.4 7.0 conditional.6
  273.2 3.1 convolution_add_fusion
  282.6 7.0 conditional.6
  286.4 3.1 convolution_add_fusion
  291.6 7.0 conditional.6
  295.4 3.1 convolution_add_fusion
  304.8 7.0 conditional.6
  308.6 3.1 convolution_add_fusion
  313.7 7.0 conditional.6
  320.7 391.2 %while.43 = (s32[]{:T(128)}, f32[256,8]{0,1:T(8,128)S(1)}, f32[256,8]{0,1:T(8,128)S(1)}, f32[256,8,128]{2,0,1:T(8,128)}, s32[32]{0:T(128)S(1)}, /*index=5*/s32[]...) while((s32[]{:T(128)}, f32[256,8]{0,1:T(8,128)S(1)}, ...), condition=%wide.region_12.13_spmd.clone, body=%wide.region_7.12_spmd.clone.sunk | while | flops 549919168 | bytes 33696912 | solution.py:148
  326.7 12.4 %conditional.7 = ((f32[256,8]{0,1:T(8,128)S(1)}, f32[256,8]{0,1:T(8,128)S(1)}, f32[256,8,128]{2,0,1:T(8,128)})) conditional(s32[]{:T(128)} %convert_element_type.79, (f32[256,8]{0,1:T(8,128)S(1)}, f32[256,8]{0,1:T(8,128)S(1)}, f32[256,8,128]{2,0,1:T(8,128)}) %tuple.141, (s32[]{:T(128)}, pred[32,512]{1,0:T(8,128)(4,1)S(1)}, s32[]{:T(128)}, s32[]{:T(128)}, ...), branch_computations={%region_8.8_spmd, %region_9.11_spmd} | conditional | flops 549919104 | bytes 33695040 | solution.py:146
  334.3 4.9 fusion.26
  345.1 12.4 %conditional.7 = ((f32[256,8]{0,1:T(8,128)S(1)}, f32[256,8]{0,1:T(8,128)S(1)}, f32[256,8,128]{2,0,1:T(8,128)})) conditional(s32[]{:T(128)} %convert_element_type.79, (f32[256,8]{0,1:T(8,128)S(1)}, f32[256,8]{0,1:T(8,128)S(1)}, f32[256,8,128]{2,0,1:T(8,128)}) %tuple.141, (s32[]{:T(128)}, pred[32,512]{1,0:T(8,128)(4,1)S(1)}, s32[]{:T(128)}, s32[]{:T(128)}, ...), branch_computations={%region_8.8_spmd, %region_9.11_spmd} | conditional | flops 549919104 | bytes 33695040 | solution.py:146
  352.7 4.9 fusion.26
  363.6 12.4 %conditional.7 = ((f32[256,8]{0,1:T(8,128)S(1)}, f32[256,8]{0,1:T(8,128)S(1)}, f32[256,8,128]{2,0,1:T(8,128)})) conditional(s32[]{:T(128)} %convert_element_type.79, (f32[256,8]{0,1:T(8,128)S(1)}, f32[256,8]{0,1:T(8,128)S(1)}, f32[256,8,128]{2,0,1:T(8,128)}) %tuple.141, (s32[]{:T(128)}, pred[32,512]{1,0:T(8,128)(4,1)S(1)}, s32[]{:T(128)}, s32[]{:T(128)}, ...), branch_computations={%region_8.8_spmd, %region_9.11_spmd} | conditional | flops 549919104 | bytes 33695040 | solution.py:146
  371.1 4.9 fusion.26
  382.0 12.4 %conditional.7 = ((f32[256,8]{0,1:T(8,128)S(1)}, f32[256,8]{0,1:T(8,128)S(1)}, f32[256,8,128]{2,0,1:T(8,128)})) conditional(s32[]{:T(128)} %convert_element_type.79, (f32[256,8]{0,1:T(8,128)S(1)}, f32[256,8]{0,1:T(8,128)S(1)}, f32[256,8,128]{2,0,1:T(8,128)}) %tuple.141, (s32[]{:T(128)}, pred[32,512]{1,0:T(8,128)(4,1)S(1)}, s32[]{:T(128)}, s32[]{:T(128)}, ...), branch_computations={%region_8.8_spmd, %region_9.11_spmd} | conditional | flops 549919104 | bytes 33695040 | solution.py:146
  389.5 4.9 fusion.26
  400.4 12.4 %conditional.7 = ((f32[256,8]{0,1:T(8,128)S(1)}, f32[256,8]{0,1:T(8,128)S(1)}, f32[256,8,128]{2,0,1:T(8,128)})) conditional(s32[]{:T(128)} %convert_element_type.79, (f32[256,8]{0,1:T(8,128)S(1)}, f32[256,8]{0,1:T(8,128)S(1)}, f32[256,8,128]{2,0,1:T(8,128)}) %tuple.141, (s32[]{:T(128)}, pred[32,512]{1,0:T(8,128)(4,1)S(1)}, s32[]{:T(128)}, s32[]{:T(128)}, ...), branch_computations={%region_8.8_spmd, %region_9.11_spmd} | conditional | flops 549919104 | bytes 33695040 | solution.py:146
  407.9 4.9 fusion.26
  418.8 12.4 %conditional.7 = ((f32[256,8]{0,1:T(8,128)S(1)}, f32[256,8]{0,1:T(8,128)S(1)}, f32[256,8,128]{2,0,1:T(8,128)})) conditional(s32[]{:T(128)} %convert_element_type.79, (f32[256,8]{0,1:T(8,128)S(1)}, f32[256,8]{0,1:T(8,128)S(1)}, f32[256,8,128]{2,0,1:T(8,128)}) %tuple.141, (s32[]{:T(128)}, pred[32,512]{1,0:T(8,128)(4,1)S(1)}, s32[]{:T(128)}, s32[]{:T(128)}, ...), branch_computations={%region_8.8_spmd, %region_9.11_spmd} | conditional | flops 549919104 | bytes 33695040 | solution.py:146
  426.3 4.9 fusion.26
  467.4 12.4 %conditional.7 = ((f32[256,8]{0,1:T(8,128)S(1)}, f32[256,8]{0,1:T(8,128)S(1)}, f32[256,8,128]{2,0,1:T(8,128)})) conditional(s32[]{:T(128)} %convert_element_type.79, (f32[256,8]{0,1:T(8,128)S(1)}, f32[256,8]{0,1:T(8,128)S(1)}, f32[256,8,128]{2,0,1:T(8,128)}) %tuple.141, (s32[]{:T(128)}, pred[32,512]{1,0:T(8,128)(4,1)S(1)}, s32[]{:T(128)}, s32[]{:T(128)}, ...), branch_computations={%region_8.8_spmd, %region_9.11_spmd} | conditional | flops 549919104 | bytes 33695040 | solution.py:146
  474.9 4.9 fusion.26
  491.8 12.4 %conditional.7 = ((f32[256,8]{0,1:T(8,128)S(1)}, f32[256,8]{0,1:T(8,128)S(1)}, f32[256,8,128]{2,0,1:T(8,128)})) conditional(s32[]{:T(128)} %convert_element_type.79, (f32[256,8]{0,1:T(8,128)S(1)}, f32[256,8]{0,1:T(8,128)S(1)}, f32[256,8,128]{2,0,1:T(8,128)}) %tuple.141, (s32[]{:T(128)}, pred[32,512]{1,0:T(8,128)(4,1)S(1)}, s32[]{:T(128)}, s32[]{:T(128)}, ...), branch_computations={%region_8.8_spmd, %region_9.11_spmd} | conditional | flops 549919104 | bytes 33695040 | solution.py:146
  499.4 4.9 fusion.26
  510.3 12.4 %conditional.7 = ((f32[256,8]{0,1:T(8,128)S(1)}, f32[256,8]{0,1:T(8,128)S(1)}, f32[256,8,128]{2,0,1:T(8,128)})) conditional(s32[]{:T(128)} %convert_element_type.79, (f32[256,8]{0,1:T(8,128)S(1)}, f32[256,8]{0,1:T(8,128)S(1)}, f32[256,8,128]{2,0,1:T(8,128)}) %tuple.141, (s32[]{:T(128)}, pred[32,512]{1,0:T(8,128)(4,1)S(1)}, s32[]{:T(128)}, s32[]{:T(128)}, ...), branch_computations={%region_8.8_spmd, %region_9.11_spmd} | conditional | flops 549919104 | bytes 33695040 | solution.py:146
  517.8 4.9 fusion.26
  540.7 12.4 %conditional.7 = ((f32[256,8]{0,1:T(8,128)S(1)}, f32[256,8]{0,1:T(8,128)S(1)}, f32[256,8,128]{2,0,1:T(8,128)})) conditional(s32[]{:T(128)} %convert_element_type.79, (f32[256,8]{0,1:T(8,128)S(1)}, f32[256,8]{0,1:T(8,128)S(1)}, f32[256,8,128]{2,0,1:T(8,128)}) %tuple.141, (s32[]{:T(128)}, pred[32,512]{1,0:T(8,128)(4,1)S(1)}, s32[]{:T(128)}, s32[]{:T(128)}, ...), branch_computations={%region_8.8_spmd, %region_9.11_spmd} | conditional | flops 549919104 | bytes 33695040 | solution.py:146
  548.3 4.9 fusion.26
  559.2 12.4 %conditional.7 = ((f32[256,8]{0,1:T(8,128)S(1)}, f32[256,8]{0,1:T(8,128)S(1)}, f32[256,8,128]{2,0,1:T(8,128)})) conditional(s32[]{:T(128)} %convert_element_type.79, (f32[256,8]{0,1:T(8,128)S(1)}, f32[256,8]{0,1:T(8,128)S(1)}, f32[256,8,128]{2,0,1:T(8,128)}) %tuple.141, (s32[]{:T(128)}, pred[32,512]{1,0:T(8,128)(4,1)S(1)}, s32[]{:T(128)}, s32[]{:T(128)}, ...), branch_computations={%region_8.8_spmd, %region_9.11_spmd} | conditional | flops 549919104 | bytes 33695040 | solution.py:146
  566.7 4.9 fusion.26
  577.6 12.4 %conditional.7 = ((f32[256,8]{0,1:T(8,128)S(1)}, f32[256,8]{0,1:T(8,128)S(1)}, f32[256,8,128]{2,0,1:T(8,128)})) conditional(s32[]{:T(128)} %convert_element_type.79, (f32[256,8]{0,1:T(8,128)S(1)}, f32[256,8]{0,1:T(8,128)S(1)}, f32[256,8,128]{2,0,1:T(8,128)}) %tuple.141, (s32[]{:T(128)}, pred[32,512]{1,0:T(8,128)(4,1)S(1)}, s32[]{:T(128)}, s32[]{:T(128)}, ...), branch_computations={%region_8.8_spmd, %region_9.11_spmd} | conditional | flops 549919104 | bytes 33695040 | solution.py:146
  585.1 4.9 fusion.26
  614.1 12.4 %conditional.7 = ((f32[256,8]{0,1:T(8,128)S(1)}, f32[256,8]{0,1:T(8,128)S(1)}, f32[256,8,128]{2,0,1:T(8,128)})) conditional(s32[]{:T(128)} %convert_element_type.79, (f32[256,8]{0,1:T(8,128)S(1)}, f32[256,8]{0,1:T(8,128)S(1)}, f32[256,8,128]{2,0,1:T(8,128)}) %tuple.141, (s32[]{:T(128)}, pred[32,512]{1,0:T(8,128)(4,1)S(1)}, s32[]{:T(128)}, s32[]{:T(128)}, ...), branch_computations={%region_8.8_spmd, %region_9.11_spmd} | conditional | flops 549919104 | bytes 33695040 | solution.py:146
  621.7 4.9 fusion.26
  632.5 12.4 %conditional.7 = ((f32[256,8]{0,1:T(8,128)S(1)}, f32[256,8]{0,1:T(8,128)S(1)}, f32[256,8,128]{2,0,1:T(8,128)})) conditional(s32[]{:T(128)} %convert_element_type.79, (f32[256,8]{0,1:T(8,128)S(1)}, f32[256,8]{0,1:T(8,128)S(1)}, f32[256,8,128]{2,0,1:T(8,128)}) %tuple.141, (s32[]{:T(128)}, pred[32,512]{1,0:T(8,128)(4,1)S(1)}, s32[]{:T(128)}, s32[]{:T(128)}, ...), branch_computations={%region_8.8_spmd, %region_9.11_spmd} | conditional | flops 549919104 | bytes 33695040 | solution.py:146
  640.1 4.9 fusion.26
  657.0 12.4 %conditional.7 = ((f32[256,8]{0,1:T(8,128)S(1)}, f32[256,8]{0,1:T(8,128)S(1)}, f32[256,8,128]{2,0,1:T(8,128)})) conditional(s32[]{:T(128)} %convert_element_type.79, (f32[256,8]{0,1:T(8,128)S(1)}, f32[256,8]{0,1:T(8,128)S(1)}, f32[256,8,128]{2,0,1:T(8,128)}) %tuple.141, (s32[]{:T(128)}, pred[32,512]{1,0:T(8,128)(4,1)S(1)}, s32[]{:T(128)}, s32[]{:T(128)}, ...), branch_computations={%region_8.8_spmd, %region_9.11_spmd} | conditional | flops 549919104 | bytes 33695040 | solution.py:146
  664.5 4.9 fusion.26
  675.4 12.4 %conditional.7 = ((f32[256,8]{0,1:T(8,128)S(1)}, f32[256,8]{0,1:T(8,128)S(1)}, f32[256,8,128]{2,0,1:T(8,128)})) conditional(s32[]{:T(128)} %convert_element_type.79, (f32[256,8]{0,1:T(8,128)S(1)}, f32[256,8]{0,1:T(8,128)S(1)}, f32[256,8,128]{2,0,1:T(8,128)}) %tuple.141, (s32[]{:T(128)}, pred[32,512]{1,0:T(8,128)(4,1)S(1)}, s32[]{:T(128)}, s32[]{:T(128)}, ...), branch_computations={%region_8.8_spmd, %region_9.11_spmd} | conditional | flops 549919104 | bytes 33695040 | solution.py:146
  682.9 4.9 fusion.26
  (603 shorter events, 215.3 us)
Async XLA Ops:
  7.2 39.6 %all-gather.4.cloned.1.call-start = ((), (), s32[]{:S(2)}) async-start(), calls=%async_computation | async-start | bytes 4718592 | tf_op jit(solution)/shard_map/all_gather | solution.py:63
  7.9 127.9 %all-gather.6.cloned.1.call-start = ((), (), s32[]{:S(2)}) async-start(), calls=%async_computation.1 | async-start | bytes 4325376 | tf_op jit(solution)/shard_map/all_gather | solution.py:86
  10.6 43.1 %copy-start.3 = (s32[32]{0:T(128)S(1)}, s32[32]{0:T(128)}, u32[]{:S(2)}) copy-start(s32[32]{0:T(128)} %param.23) | copy-start | bytes 388
  10.6 43.7 %copy-start.1 = (bf16[256,1024]{1,0:T(8,128)(2,1)S(1)}, bf16[256,1024]{1,0:T(8,128)(2,1)}, u32[]{:S(2)}) copy-start(bf16[256,1024]{1,0:T(8,128)(2,1)} %param.18) | copy-start | bytes 1572868
  10.6 45.0 %copy-start.2 = (s32[32,256]{1,0:T(8,128)S(1)}, s32[32,256]{1,0:T(8,128)}, u32[]{:S(2)}) copy-start(s32[32,256]{1,0:T(8,128)} %param.22) | copy-start | bytes 98308
  53.0 267.7 %all-gather.8.cloned.1.call-start = ((), (), s32[]{:S(2)}) async-start(), calls=%async_computation.2 | async-start | bytes 8650752 | tf_op jit(solution)/shard_map/all_gather | solution.py:116
  60.3 83.1 %copy-start.4 = (s32[32]{0:T(128)S(1)}, s32[32]{0:T(128)}, u32[]{:S(2)}) copy-start(s32[32]{0:T(128)} %param.21) | copy-start | bytes 388
  143.3 177.4 %copy-start.5 = (s32[32]{0:T(128)S(1)}, s32[32]{0:T(128)}, u32[]{:S(2)}) copy-start(s32[32]{0:T(128)} %param.20) | copy-start | bytes 388
  331.4 2.0 copy-start
  349.8 2.0 copy-start
  368.3 2.0 copy-start
  386.7 2.0 copy-start
  405.1 2.0 copy-start
  423.5 2.0 copy-start
  472.1 2.0 copy-start
  496.5 2.0 copy-start
  515.0 2.0 copy-start
  545.4 2.0 copy-start
  563.9 2.0 copy-start
  582.3 2.0 copy-start
  618.8 2.0 copy-start
  637.2 2.0 copy-start
  661.7 2.0 copy-start
  680.1 2.0 copy-start
Sparse Core Ops, SparseCore 0:
  9.8 36.8 all-gather.3
  53.1 82.6 all-gather.5
  138.4 95.9 all-gather.7
where the time goes:
time: 726 us; the launch traced here: 721 us
  loops' own time  258 us (36%)
  matrix products  168 us (23%)
  waiting for transfers between devices  113 us (16%)
  local copies, waits for them, and re-layouts  113 us (16%)
  other arithmetic  53.4 us (7%)
  between operations  15.2 us (2%)
    another operation x1, loops' own time, shards(): state = lax.fori_loop(0, count // over_block, step, state)  152 us
    dot_general x32, matrix products, attend(): jnp.einsum('rqn,nd->rqd', weights.astype(jnp.bfloat16), vals, preferred_e...  128 us
    all_gather x1, waiting for transfers between devices, shards(): piece = lax.all_gather(fresh, 'ctx', axis=0, tiled=True)  75.5 us
    another operation x64, loops' own time, step(): return lax.cond(visible, attend_block, keep_state, inner)  61.7 us
    another operation x1, loops' own time, shards(): state = lax.fori_loop(0, count // block, step, state)  44.6 us
    dynamic_slice x64, local copies, waits for them, and re-layouts, step(): place = span_place[span]  42.5 us
    all_gather x1, waiting for transfers between devices, shards(): lax.all_gather(hidden_rows, 'head', axis=1, tiled=True)  36.1 us
    dot_general x32, matrix products, attend(): jnp.einsum('rqd,nd->rqn', query_blocks, keys, preferred_element_type=jnp....  34.5 us
  transfers between devices with their start and end apart: 3, of which 2 were waited for; matrix products, arithmetic and copies ran while one was open for 18% of the time, Pallas kernels for 0%

commit v1 on v0

v1 whole, which is shorter than its diff:
```python
import functools
import math

import jax
import jax.numpy as jnp
import numpy as np
from jax import lax
from jax.experimental import pallas as pl
from jax.experimental.pallas import tpu as pltpu
from jax.sharding import PartitionSpec as P

BLK = 128
LANES = 256


def rope_freqs(size):
    half = size // 2
    base = 500000.0 ** (-2.0 * jnp.arange(half, dtype=jnp.float32) / size)
    wavelen = 2.0 * math.pi / base
    smooth = (8192.0 / wavelen - 1.0) / 3.0
    blended = (1.0 - smooth) * base / 8.0 + smooth * base
    return jnp.where(wavelen < 2048.0, base, jnp.where(wavelen > 8192.0, base / 8.0, blended))


def rope_table(positions, size):
    angles = positions.astype(jnp.float32)[:, None] * rope_freqs(size)[None, :]
    cosine, sine = jnp.cos(angles), jnp.sin(angles)
    return jnp.stack(
        [jnp.concatenate([cosine, cosine], 1), jnp.concatenate([-sine, sine], 1)], axis=1
    )


def rotate(keys, cosine, sine):
    return keys * cosine + pltpu.roll(keys, keys.shape[-1] // 2, 1) * sine


def project_kernel(hid_ref, weight_ref, turn_ref, out_ref, acc_ref):
    part = jnp.dot(hid_ref[0], weight_ref[...], preferred_element_type=jnp.float32)
    step = pl.program_id(0)

    @pl.when(step == 0)
    def _():
        acc_ref[...] = part

    @pl.when(step > 0)
    def _():
        acc_ref[...] += part

    @pl.when(step == pl.num_programs(0) - 1)
    def _():
        width = acc_ref.shape[1] // 2
        keys = rotate(acc_ref[:, :width], turn_ref[:, 0], turn_ref[:, 1])
        out_ref[:, :width] = keys.astype(out_ref.dtype)
        out_ref[:, width:] = acc_ref[:, width:].astype(out_ref.dtype)


def project(gathered, weight, turn):
    chunks, rows, depth = gathered.shape
    cols = weight.shape[1]
    return pl.pallas_call(
        project_kernel,
        grid=(chunks,),
        in_specs=[
            pl.BlockSpec((1, rows, depth), lambda i: (i, 0, 0)),
            pl.BlockSpec((depth, cols), lambda i: (i, 0)),
            pl.BlockSpec(turn.shape, lambda i: (0, 0, 0)),
        ],
        out_specs=pl.BlockSpec((rows, cols), lambda i: (0, 0)),
        out_shape=jax.ShapeDtypeStruct((rows, cols), jnp.bfloat16),
        scratch_shapes=[pltpu.VMEM((rows, cols), jnp.float32)],
        name="project",
    )(gathered, weight, turn)


def attend_kernel(
    slot_ref,
    place_ref,
    count_ref,
    me_ref,
    q_ref,
    rows_ref,
    turn_ref,
    pool_ref,
    fresh_ref,
    out_ref,
    by_place,
    owner_of,
    pool_buf,
    fresh_buf,
    q_scr,
    k_scr,
    v_scr,
    acc_scr,
    max_scr,
    sum_scr,
    sems,
):
    spans, rows = rows_ref.shape
    span_len = pool_buf.shape[1]
    width = pool_buf.shape[2] // 2
    heads = q_ref.shape[1] // width
    per = LANES // BLK
    tiles_per_block = heads // per
    log2e = 1.4426950408889634
    factor = width**-0.5 * log2e
    me = me_ref[0]
    mine = (me // 2) % 2
    my_place = place_ref[me]
    my_blocks = count_ref[me]
    n_tiles = my_blocks * tiles_per_block

    def fill(s, carry):
        owner_of[slot_ref[s]] = s

        @pl.when((s // 2) % 2 == mine)
        def _():
            by_place[place_ref[s]] = s

        return carry

    lax.fori_loop(0, spans, fill, 0)

    def at_step(i):
        return by_place[jnp.where(i == 0, my_place, i - 1)]

    def copies(i, slot):
        span = at_step(i)
        return (
            pltpu.make_async_copy(
                pool_ref.at[owner_of[span]], pool_buf.at[slot], sems.at[0, slot]
            ),
            pltpu.make_async_copy(
                fresh_ref.at[(span // 4) * 2 + span % 2], fresh_buf.at[slot], sems.at[1, slot]
            ),
        )

    for c in copies(0, 0):
        c.start()

    for b in range(rows // BLK):
        for h in range(heads):
            piece = q_ref[b * BLK : (b + 1) * BLK, h * width : (h + 1) * width]
            j = b * tiles_per_block + h // per
            lo = (h % per) * BLK
            q_scr[j, :, lo : lo + BLK] = piece.T

    def prepare(i, slot):
        span = at_step(i)
        place = place_ref[span]
        live = count_ref[span] * BLK
        picks = rows_ref[pl.ds(span, 1), :]
        picks = jnp.where(lax.broadcasted_iota(jnp.int32, (1, rows), 1) < live, picks, -1)
        here = lax.broadcasted_iota(jnp.int32, (span_len, rows), 0)
        chosen = (here == picks).astype(jnp.float32)
        replaced = jnp.sum(chosen, axis=1, keepdims=True) > 0.5
        chosen = chosen.astype(jnp.bfloat16)
        moved = jnp.dot(chosen, fresh_buf[slot], preferred_element_type=jnp.float32)
        cached = pool_buf[slot].astype(jnp.float32)
        turn = turn_ref[place]
        keys = rotate(cached[:, :width], turn[0:1], turn[1:2])
        k_scr[...] = jnp.where(replaced, moved[:, :width], keys).astype(jnp.bfloat16)
        vals = jnp.where(replaced, moved[:, width:], cached[:, width:])
        v_scr[...] = vals.T.astype(jnp.bfloat16)

    def step(i, diagonal):
        slot = lax.rem(i, 2)

        @pl.when(i < my_place)
        def _():
            for c in copies(i + 1, 1 - slot):
                c.start()

        for c in copies(i, slot):
            c.wait()
        prepare(i, slot)

        def tile(j, carry):
            scores = jnp.dot(k_scr[...], q_scr[j], preferred_element_type=jnp.float32)
            if diagonal:
                block = j // tiles_per_block
                limit = rows_ref[pl.ds(me, 1), :]
                limit = jnp.where(block == 0, limit[:, :BLK], limit[:, BLK:])
                limit = jnp.concatenate([limit] * per, axis=1)
                here = lax.broadcasted_iota(jnp.int32, scores.shape, 0)
                scores = jnp.where(here <= limit, scores, -1e30)
                largest = jnp.max(scores, axis=0, keepdims=True)
            else:
                old = max_scr[j]
                largest = jnp.maximum(old, jnp.max(scores, axis=0, keepdims=True))
            weights = jnp.exp2((scores - largest) * factor)
            total = jnp.sum(weights, axis=0, keepdims=True)
            mixed = jnp.dot(
                v_scr[...], weights.astype(jnp.bfloat16), preferred_element_type=jnp.float32
            )
            if diagonal:
                sum_scr[j] = total
                acc_scr[j] = mixed
            else:
                shrink = jnp.exp2((old - largest) * factor)
                sum_scr[j] = sum_scr[j] * shrink + total
                acc_scr[j] = acc_scr[j] * shrink + mixed
            max_scr[j] = largest
            return carry

        def group(g, carry):
            for k in range(tiles_per_block):
                tile(g * tiles_per_block + k, 0)
            return carry

        lax.fori_loop(0, my_blocks, group, 0)

    step(0, True)

    def rest(i, carry):
        step(i, False)
        return carry

    lax.fori_loop(1, my_place + 1, rest, 0)

    for b in range(rows // BLK):

        @pl.when(b < my_blocks)
        def _():
            for h in range(heads):
                j = b * tiles_per_block + h // per
                lo = (h % per) * BLK
                piece = acc_scr[j, :, lo : lo + BLK] / sum_scr[j, :, lo : lo + BLK]
                out_ref[b * BLK : (b + 1) * BLK, h * width : (h + 1) * width] = piece.T.astype(
                    out_ref.dtype
                )

        @pl.when(b >= my_blocks)
        def _():
            out_ref[b * BLK : (b + 1) * BLK, :] = jnp.zeros(
                (BLK, heads * width), out_ref.dtype
            )


def attend(slot_span, span_place, block_count, me, queries, row_index, turn, pool, fresh):
    spans, span_len, both = pool.shape
    rows = fresh.shape[1]
    width = both // 2
    heads = queries.shape[1] // width
    tiles = rows * heads // LANES
    smem = pl.BlockSpec(memory_space=pltpu.SMEM)
    vmem = pl.BlockSpec(memory_space=pltpu.VMEM)
    hbm = pl.BlockSpec(memory_space=pl.ANY)
    return pl.pallas_call(
        attend_kernel,
        in_specs=[smem, smem, smem, smem, vmem, vmem, vmem, hbm, hbm],
        out_specs=vmem,
        out_shape=jax.ShapeDtypeStruct(queries.shape, queries.dtype),
        scratch_shapes=[
            pltpu.SMEM((spans,), jnp.int32),
            pltpu.SMEM((spans,), jnp.int32),
            pltpu.VMEM((2, span_len, both), jnp.bfloat16),
            pltpu.VMEM((2, rows, both), jnp.bfloat16),
            pltpu.VMEM((tiles, width, LANES), jnp.bfloat16),
            pltpu.VMEM((span_len, width), jnp.bfloat16),
            pltpu.VMEM((width, span_len), jnp.bfloat16),
            pltpu.VMEM((tiles, width, LANES), jnp.float32),
            pltpu.VMEM((tiles, 1, LANES), jnp.float32),
            pltpu.VMEM((tiles, 1, LANES), jnp.float32),
            pltpu.SemaphoreType.DMA((2, 2)),
        ],
        compiler_params=pltpu.CompilerParams(vmem_limit_bytes=40 * 1024 * 1024),
        name="attend",
    )(slot_span, span_place, block_count, me, queries, row_index, turn, pool, fresh)


def shards(hidden_rows, kv_weight, queries, kv_pool, slot_span, span_place, row_index, block_count):
    width = kv_weight.shape[1] // 2
    span_len = kv_pool.shape[0]
    spans = span_place.shape[0]
    position = lax.axis_index("ctx")
    my_pos = span_place[position] * span_len + lax.dynamic_index_in_dim(
        row_index, position, 0, keepdims=False
    )
    groups = [[c for c in range(spans) if c // 2 % 2 == q] for q in range(2)]
    gathered = lax.all_gather(hidden_rows, "head", axis=0)
    fresh = project(gathered, kv_weight, rope_table(my_pos, width))
    all_fresh = lax.all_gather(fresh, "ctx", axis=0, axis_index_groups=groups)
    all_pool = lax.all_gather(kv_pool, "ctx", axis=0)
    turn = rope_table(jnp.arange(spans // 2, dtype=jnp.int32) * span_len, width)
    attended = attend(
        slot_span,
        span_place,
        block_count,
        position.astype(jnp.int32).reshape(1),
        queries,
        row_index,
        turn,
        all_pool,
        all_fresh,
    )
    return fresh, attended


def solution(mesh):
    in_specs = (
        P("ctx", "head"),
        P(None, "head"),
        P("ctx", "head"),
        P("ctx", "head"),
        P(),
        P(),
        P(),
        P(),
    )
    out_specs = (P("ctx", "head"), P("ctx", "head"))
    return jax.shard_map(shards, mesh=mesh, in_specs=in_specs, out_specs=out_specs, check_vma=False)
```

time: 726 us -> 302 us (0.42)
  the two profiles are of different devices: /device:TPU:70 before, /device:TPU:224 now
where the time goes in v1:
time: 302 us; the launch traced here: 301 us
  waiting for transfers between devices  203 us (67%)
  Pallas kernels  74 us (25%)
  between operations  14.5 us (5%)
  local copies, waits for them, and re-layouts  6.23 us (2%)
    all_gather x1, waiting for transfers between devices, shards(): all_pool = lax.all_gather(kv_pool, 'ctx', axis=0)  98.2 us
    all_gather x1, waiting for transfers between devices, shards(): all_fresh = lax.all_gather(fresh, 'ctx', axis=0, axis_index_groups=groups)  71 us
    pallas_call x1, Pallas kernels, attend(): pl.pallas_call(attend_kernel, in_specs=[smem, smem, smem, smem, vmem, vme...  66.3 us
    all_gather x1, waiting for transfers between devices, shards(): gathered = lax.all_gather(hidden_rows, 'head', axis=0)  32.8 us
    pallas_call x1, Pallas kernels, project(): pl.pallas_call(project_kernel, grid=(chunks,), in_specs=[pl.BlockSpec((1,...  7.66 us
  transfers between devices with their start and end apart: 3, of which 3 were waited for; matrix products, arithmetic and copies ran while one was open for 1% of the time, Pallas kernels for 0%

profile of v1, /device:TPU:224, one launch (start us, length us, event | category | flops | bytes accessed | tf_op | source)
XLA Modules:
  0.0 300.8 jit_solution(4992550303977631691)
XLA Ops:
  7.2 0.0 all-gather.7.cloned.1.call-start
  7.2 0.7 all-gather.7.cloned.1.call-update
  7.9 0.0 all-gather.11.cloned.1.call-start
  7.9 1.2 dynamic_slice.7
  9.9 0.7 add_convert_fusion
  10.6 0.5 multiply_cosine_fusion
  11.1 0.1 pad_maximum_fusion.1
  11.3 0.9 pad_maximum_fusion.turn_ref
  12.2 32.8 %all-gather.7.cloned.1.call-done = bf16[2048,1024]{1,0:T(8,128)(2,1)} async-done(((bf16[256,1024]{1,0:T(8,128)(2,1)}), bf16[2048,1024]{1,0:T(8,128)(2,1)}) %all-gather.7.cloned.1.call-update) | async-done | bytes 4194320 | tf_op jit(solution)/shard_map/all_gather | solution.py:280
  45.0 0.0 copy-start.2
  45.0 0.0 copy-start.3
  45.0 0.0 copy-start.4
  45.0 0.0 copy-start.5
  45.0 0.0 copy-start.6
  45.0 7.7 %project.1 = bf16[256,256]{1,0:T(8,128)(2,1)} custom-call(bf16[8,256,1024]{2,1,0:T(8,128)(2,1)} %bitcast.16, bf16[8192,256]{1,0:T(8,128)(2,1)} %weight_ref.1, f32[256,2,128]{2,1,0:T(2,128)} %pad_maximum_fusion.turn_ref), custom_call_target="tpu_custom_call" | custom-call | tf_op jit(solution)/shard_map/project/pallas_call | solution.py:60
  52.7 0.0 all-gather.11.cloned.1.call-update
  52.7 0.0 all-gather.9.cloned.1.call-start
  52.8 0.7 all-gather.9.cloned.1.call-update
  53.5 0.1 multiply_cosine_fusion.1
  53.6 0.1 pad_maximum_fusion.4
  53.7 71.0 %all-gather.11.cloned.1.call-done = bf16[4096,256]{1,0:T(8,128)(2,1)} async-done(((bf16[256,256]{1,0:T(8,128)(2,1)}), bf16[4096,256]{1,0:T(8,128)(2,1)}) %all-gather.11.cloned.1.call-update) | async-done | bytes 2097168 | tf_op jit(solution)/shard_map/all_gather | solution.py:282
  124.6 98.2 %all-gather.9.cloned.1.call-done = bf16[16384,256]{1,0:T(8,128)(2,1)} async-done(((bf16[512,256]{1,0:T(8,128)(2,1)}), bf16[16384,256]{1,0:T(8,128)(2,1)}) %all-gather.9.cloned.1.call-update) | async-done | bytes 8388624 | tf_op jit(solution)/shard_map/all_gather | solution.py:283
  222.9 0.0 copy-done.2
  222.9 0.0 copy-done.3
  222.9 0.0 copy-done.4
  222.9 0.0 copy-done.5
  222.9 0.0 copy-done.6
  222.9 0.0 copy-start
  222.9 3.4 %copy-done = bf16[16384,256]{1,0:T(8,128)(2,1)S(1)} copy-done((bf16[16384,256]{1,0:T(8,128)(2,1)S(1)}, bf16[16384,256]{1,0:T(8,128)(2,1)}, u32[]{:S(2)}) %copy-start) | copy-done | bytes 8388632
  226.3 0.0 copy-start.1
  226.3 1.6 copy-done.1
  227.9 66.3 %attend.1 = bf16[256,1024]{1,0:T(8,128)(2,1)} custom-call(s32[32]{0:T(128)S(1)} %copy-done.5, s32[32]{0:T(128)S(1)} %copy-done.4, s32[32]{0:T(128)S(1)} %copy-done.6, s32[1]{0:T(128)} %bitcast.6.me_ref, bf16[256,1024]{1,0:T(8,128)(2,1)S(1)} %copy-done.2, s32[32,256]{1,0:T(8,128)S(1)} %copy-done.3, f32[16,2,128]{2,1,0:T(2,128)S(1)} %pad_maximum_fusion.3.turn_ref, ...), custom_call_target="tpu_custom_call" | custom-call | tf_op jit(solution)/shard_map/attend/pallas_call | solution.py:248
  (3 shorter events, 0.0 us)
Async XLA Ops:
  7.2 37.8 %all-gather.7.cloned.1.call-start = ((), (), s32[]{:S(2)}) async-start(), calls=%async_computation | async-start | bytes 4718592 | tf_op jit(solution)/shard_map/all_gather | solution.py:280
  7.9 116.7 %all-gather.11.cloned.1.call-start = ((), (), s32[]{:S(2)}) async-start(), calls=%async_computation.2 | async-start | bytes 2228224 | tf_op jit(solution)/shard_map/all_gather | solution.py:282
  45.0 177.9 %copy-start.2 = (bf16[256,1024]{1,0:T(8,128)(2,1)S(1)}, bf16[256,1024]{1,0:T(8,128)(2,1)}, u32[]{:S(2)}) copy-start(bf16[256,1024]{1,0:T(8,128)(2,1)} %q_ref.1) | copy-start | bytes 1572868
  45.0 177.9 %copy-start.3 = (s32[32,256]{1,0:T(8,128)S(1)}, s32[32,256]{1,0:T(8,128)}, u32[]{:S(2)}) copy-start(s32[32,256]{1,0:T(8,128)} %rows_ref.1) | copy-start | bytes 98308
  45.0 177.9 %copy-start.4 = (s32[32]{0:T(128)S(1)}, s32[32]{0:T(128)}, u32[]{:S(2)}) copy-start(s32[32]{0:T(128)} %place_ref.1) | copy-start | bytes 388
  45.0 177.9 %copy-start.5 = (s32[32]{0:T(128)S(1)}, s32[32]{0:T(128)}, u32[]{:S(2)}) copy-start(s32[32]{0:T(128)} %slot_ref.1) | copy-start | bytes 388
  45.0 177.9 %copy-start.6 = (s32[32]{0:T(128)S(1)}, s32[32]{0:T(128)}, u32[]{:S(2)}) copy-start(s32[32]{0:T(128)} %count_ref.1) | copy-start | bytes 388
  52.7 170.2 %all-gather.9.cloned.1.call-start = ((), (), s32[]{:S(2)}) async-start(), calls=%async_computation.1 | async-start | bytes 8650752 | tf_op jit(solution)/shard_map/all_gather | solution.py:283
  222.9 3.4 %copy-start = (bf16[16384,256]{1,0:T(8,128)(2,1)S(1)}, bf16[16384,256]{1,0:T(8,128)(2,1)}, u32[]{:S(2)}) copy-start(bf16[16384,256]{1,0:T(8,128)(2,1)} %all-gather.9.cloned.1.call-done) | copy-start | bytes 25165828
  226.3 1.6 copy-start.1
Sparse Core Ops, SparseCore 0:
  9.9 35.1 all-gather.6
  52.8 71.7 all-gather.10
  127.2 95.6 all-gather.8
